TPU v7x, 256 devices: a whole 4x4x8 slice. The times are simulated.
256 devices in a mesh: layer: 4 (over x_hi, core), slab: 64 (over z, y, x_lo).
Axes of the slice: x: 4 (x_hi: 2, x_lo: 2; x = x_hi * 2 + x_lo), y: 4, z: 8, core: 2. Of those that a mesh axis runs over, the one named last changes fastest.
Arguments:
- inputs: bfloat16 [4, 128, 3584], P('layer', 'slab'), may hold values from -6 to 6
- encoder: bfloat16 [4, 3584, 8192], P('layer', None, 'slab'), may hold values from -0.09375 to 0.09375
- active: int32 [4, 128, 8192], P('layer', None, 'slab'), may hold values 0 or 1
- decoder: bfloat16 [4, 4, 8192, 3584], P('layer', None, 'slab'), may hold values from -0.0625 to 0.0625
- goals: bfloat16 [7, 128, 3584], P(None, 'slab'), may hold values from -6 to 6
Outputs:
- grad_encoder: bfloat16 [4, 3584, 8192], P('layer', None, 'slab')
- grad_decoder: bfloat16 [4, 4, 8192, 3584], P('layer', None, 'slab')
All inputs are finite; a program needn't handle non-finite values. No bound on the sum of `active` on one device may be relied on, other than what follows from the above.
Results may differ from a plain program's by a relative error of at most 0.013.
Values may be sent and summed in bfloat16 or wider, within the bound.
A program may use at most 64 MiB of HBM per device.

v0:
```python
import math

import jax
import jax.numpy as jnp
from jax import lax
from jax.sharding import PartitionSpec as P


def prefix(array, axis, combine, identity):
    devices, here = (lax.axis_size(axis), lax.axis_index(axis))
    everything = lax.all_gather(array.astype(jnp.bfloat16), axis)
    start = jnp.broadcast_to(jnp.asarray(identity, array.dtype), array.shape)

    def turn(k, before):
        reached = k < here
        new = combine(before, everything[k].astype(array.dtype))
        return jnp.where(reached, new, before)

    return lax.fori_loop(0, devices, turn, start)


def prefix_2(part, axis, combine, identity):
    count = lax.axis_size(axis)
    place = lax.axis_index(axis)
    ahead = count - 1 - place
    gathered = lax.all_gather(part, axis)
    state = jnp.zeros_like(part) + jnp.asarray(identity, part.dtype)

    def one(turn, state):
        source = count - 1 - turn
        return combine(state, lax.dynamic_index_in_dim(gathered, source, 0, False))

    return lax.fori_loop(0, ahead, one, state)


def add_parts(earlier, later):
    return earlier + later


def local(inputs, encoder, active, decoder, goals):
    layer_index = lax.axis_index("layer")
    span = decoder.shape[1]
    targets = goals.shape[0]
    tok_rows = inputs.shape[1]
    width = inputs.shape[2]
    local_rows = inputs[0]
    enc_here = encoder[0]
    dec_here = decoder[0]
    active_here = active[0].astype(jnp.float32)
    all_rows = active_here.shape[0]
    scale = 1.0 / math.sqrt(all_rows)
    gathered = lax.all_gather(local_rows, "slab", axis=0, tiled=True)
    pre = jnp.dot(gathered, enc_here, preferred_element_type=jnp.float32)
    latents = (active_here * pre).astype(jnp.bfloat16)
    lat_rows = latents
    own_terms = lax.psum_scatter(
        jnp.einsum("tf,kfd->tkd", lat_rows, dec_here, preferred_element_type=jnp.float32),
        "slab",
        scatter_dimension=0,
        tiled=True,
    )
    own_terms = jnp.transpose(own_terms, (1, 0, 2))
    blank = jnp.zeros((targets, tok_rows, width), jnp.float32)
    contrib = lax.dynamic_update_slice(blank, own_terms, (layer_index, 0, 0))
    goal_float = goals.astype(jnp.float32)
    earlier_sum = prefix(contrib, "layer", add_parts, blank)
    inclusive = earlier_sum + contrib
    err_all = ((inclusive - goal_float) * scale).astype(jnp.bfloat16)
    target_ids = jnp.arange(targets, dtype=jnp.int32)
    finished = (jnp.minimum(target_ids, span - 1) == layer_index)[:, None, None]
    err_zero = jnp.zeros((targets, tok_rows, width), jnp.bfloat16)
    err_local = jnp.where(finished, err_all, err_zero)
    later_err = prefix_2(err_local, "layer", add_parts, err_zero)
    errors = later_err + err_local
    own_err = lax.dynamic_slice_in_dim(errors, layer_index, span, 0)
    piece = lax.all_gather(own_err, "slab", axis=1, tiled=True)
    lat_rows = latents
    grad_acc = jnp.einsum("tf,ktd->kfd", lat_rows, piece, preferred_element_type=jnp.float32)
    dlat_rows = jnp.einsum("ktd,kfd->tf", piece, dec_here, preferred_element_type=jnp.float32)
    dpre = (active_here * dlat_rows).astype(jnp.bfloat16)
    grad_enc = lax.dot_general(
        gathered, dpre, (((0,), (0,)), ((), ())), preferred_element_type=jnp.float32
    )
    return (grad_enc.astype(jnp.bfloat16)[None], grad_acc.astype(jnp.bfloat16)[None])


def solution(mesh):
    return jax.shard_map(
        local,
        mesh=mesh,
        in_specs=(
            P("layer", "slab", None),
            P("layer", None, "slab"),
            P("layer", None, "slab"),
            P("layer", None, "slab", None),
            P(None, "slab", None),
        ),
        out_specs=(P("layer", None, "slab"), P("layer", None, "slab", None)),
        check_vma=False,
    )
```

profile of v0, /device:TPU:8, one launch (start us, length us, event | category | flops | bytes accessed | tf_op | source)
XLA Modules:
  0.0 1165.0 jit_solution(3818584918007336058)
XLA Ops:
  7.2 0.9 copy.18
  8.1 165.8 %all-gather = bf16[1,128,3584]{2,0,1:T(2,128)(2,1)S(1)} all-gather(bf16[1,2,3584]{2,0,1:T(2,128)(2,1)S(1)} %copy.18), channel_id=2, replica_groups=mesh['layer'=4,'slab'=64] {'slab'}, dimensions={1}, use_global_device_ids=true | all-gather | bytes 931840 | tf_op jit(solution)/shard_map/all_gather | solution.py:52
  174.0 1.2 fusion.24
  175.2 1.1 fusion.4
  176.3 7.7 copy.19
  184.2 0.6 copy-done.3
  184.7 0.6 dynamic-slice.1
  186.0 630.5 %all-reduce.3.cloned.1.call-done = f32[128,4,3584]{2,1,0:T(4,128)} async-done(((f32[128,4,3584]{2,1,0:T(4,128)}), f32[128,4,3584]{2,1,0:T(4,128)}) %all-reduce.3.cloned.1.call-update) | async-done | bytes 7340048
  816.5 0.9 dynamic-slice_bitcast_fusion
  817.6 7.7 all-gather.1
  825.3 1.0 while.31
  825.5 0.2 add_select_fusion.2
  825.8 0.2 add_select_fusion.2
  826.0 0.2 add_select_fusion.2
  826.3 1.0 dynamic-slice_add_fusion
  827.3 1.1 broadcast_select_fusion
  828.4 8.1 all-gather.2
  836.6 0.7 while.30
  837.4 0.6 copy.23
  838.1 300.7 %all-gather.5.cloned.1.call-done = bf16[4,128,3584]{2,0,1:T(4,128)(2,1)} async-done(((bf16[4,2,3584]{2,0,1:T(4,128)(2,1)}), bf16[4,128,3584]{2,0,1:T(4,128)(2,1)}) %all-gather.5.cloned.1.call-update) | async-done | bytes 3670032 | tf_op jit(solution)/shard_map/all_gather | solution.py:76
  1138.8 5.0 fusion
  1143.8 6.0 copy.27
  1149.8 6.2 fusion.1
  1156.0 2.2 copy.26
  (23 shorter events, 1.2 us)
Async XLA Ops:
  7.2 166.8 %copy-start = (bf16[1,3584,128]{2,1,0:T(8,128)(2,1)S(1)}, bf16[1,3584,128]{2,1,0:T(8,128)(2,1)}, u32[]{:S(2)}) copy-start(bf16[1,3584,128]{2,1,0:T(8,128)(2,1)} %param.10) | copy-start | bytes 2752516
  7.2 809.4 %all-reduce.3.cloned.1.call-start = ((), (), s32[]{:S(2)}) async-start(), calls=%async_computation.1 | async-start | bytes 14680064
  7.2 168.0 %copy-start.1 = (bf16[1,4,128,3584]{3,2,1,0:T(8,128)(2,1)S(1)}, bf16[1,4,128,3584]{3,2,1,0:T(8,128)(2,1)}, u32[]{:S(2)}) copy-start(bf16[1,4,128,3584]{3,2,1,0:T(8,128)(2,1)} %param.12) | copy-start | bytes 11010052
  184.0 0.7 copy-start.3
  184.1 954.7 %all-gather.5.cloned.1.call-start = ((), (), s32[]{:S(2)}) async-start(), calls=%async_computation | async-start | bytes 3727360 | tf_op jit(solution)/shard_map/all_gather | solution.py:76
  1143.8 6.0 copy-start.2
Sparse Core Ops, SparseCore 0:
  184.2 632.3 all-reduce.2
  838.2 300.5 all-gather.4
where the time goes:
time: 1170 us
  waiting for transfers between devices  931 us (80%)
  blocking collectives  182 us (16%)
  local copies, waits for them, and re-layouts  19.9 us (2%)
  between operations  14.8 us (1%)
  matrix products  13.6 us (1%)
    unnamed x3, waiting for transfers between devices  631 us
    all_gather x1, waiting for transfers between devices, local(): piece = lax.all_gather(own_err, 'slab', axis=1, tiled=True)  301 us
    all_gather x1, blocking collectives, local(): gathered = lax.all_gather(local_rows, 'slab', axis=0, tiled=True)  166 us
  transfers between devices with their start and end apart: 2, of which 2 were waited for; matrix products, arithmetic and copies ran while one was open for 0% of the time, Pallas kernels for 0%

commit v1 on v0

v1 whole, which is shorter than its diff:
```python
import math

import jax
import jax.numpy as jnp
from jax import lax
from jax.experimental import pallas as pl
from jax.experimental.pallas import tpu as pltpu
from jax.sharding import PartitionSpec as P

MESH = pl.DeviceIdType.MESH
F32, BF16 = jnp.float32, jnp.bfloat16

NZ, NG = 8, 8
TOK, D, FL = 128, 3584, 128
ROWS = 16
LANES = 128
TILES = D // LANES
NQ = 3
WIDE = 3 * LANES
XROWS = 64
MID, PAIR = 3, 2


def cols(tile, count=3):
    return pl.ds(pl.multiple_of(tile * LANES, LANES), count * LANES)


def kernel(
    inputs_ref,
    goals_ref,
    active_ref,
    enc_hbm,
    dec_hbm,
    genc_hbm,
    gdec_hbm,
    enc,
    dec,
    gdec,
    genc,
    xstage,
    xz,
    xwide,
    xb,
    xt,
    mask,
    lat_ref,
    latt_ref,
    dlat_ref,
    goal_block,
    sib_out,
    sib_in,
    part,
    part_in,
    zpart,
    zpart_in,
    xsum,
    xsum_in,
    err,
    err_sib,
    load_sem,
    out_sem,
    xz_send,
    xz_recv,
    xp_send,
    xp_recv,
    sib_send,
    sib_recv,
    part_send,
    part_recv,
    zp_send,
    zp_recv,
    xs_send,
    xs_recv,
    ez_send,
    ez_recv,
    ep_send,
    ep_recv,
    es_send,
    es_recv,
):
    layer = lax.axis_index("layer")
    slab = lax.axis_index("slab")
    x_hi, core = layer // 2, layer % 2
    z, g = slab // NG, slab % NG
    scale = 1.0 / math.sqrt(TOK)

    def z_peer(d):
        return (layer, ((z + d) % NZ) * NG + g)

    def g_peer(d):
        return (layer, z * NG + (g + d) % NG)

    sibling = (x_hi * 2 + 1 - core, slab)
    across = ((1 - x_hi) * 2 + core, slab)

    k_a = 3 * x_hi
    k_b = (layer + 2) % 4
    k_c = 3 - layer
    k_s = 1 + x_hi
    send_a = (core + x_hi + 1) % 2
    recv_a = 1 - send_a
    k_r = recv_a * k_a + (1 - recv_a) * k_b
    k_n = (1 - recv_a) * k_a + recv_a * k_b
    z_s, z_r, z_n = 5 * (1 - send_a), 5 * (1 - recv_a), 5 * recv_a

    def tile_of(zz, q, is_a):
        return 9 * zz + 3 * q - 44 * (1 - is_a)

    enc_copy = pltpu.make_async_copy(enc_hbm.at[0], enc, load_sem.at[0])
    dec_copy = pltpu.make_async_copy(dec_hbm.at[0], dec, load_sem.at[1])
    enc_copy.start()
    dec_copy.start()

    barrier = pltpu.get_barrier_semaphore()

    @pl.loop(1, 8)
    def _(d):
        pl.semaphore_signal(barrier, inc=1, device_id=z_peer(d), device_id_type=MESH)
        pl.semaphore_signal(barrier, inc=1, device_id=g_peer(d), device_id_type=MESH)

    pl.semaphore_signal(barrier, inc=1, device_id=sibling, device_id_type=MESH)
    pl.semaphore_signal(barrier, inc=1, device_id=across, device_id_type=MESH)

    xstage[...] = jnp.zeros_like(xstage)
    for c in range(TILES):
        xstage[2 * c : 2 * c + 2, :] = inputs_ref[0, :, c * LANES : (c + 1) * LANES].astype(F32)
    xz[z] = xstage[...].astype(BF16)

    pl.semaphore_wait(barrier, 16)

    def send(src, dst, ssem, rsem, device):
        pltpu.make_async_remote_copy(
            src_ref=src, dst_ref=dst, send_sem=ssem, recv_sem=rsem, device_id=device, device_id_type=MESH
        ).start()

    def wait(ref, sem):
        pltpu.make_async_copy(ref, ref, sem).wait()

    @pl.loop(1, 8)
    def _(d):
        send(xz.at[z], xz.at[z], xz_send, xz_recv, z_peer(d))

    for gg in range(NG):
        for r in range(2):
            mask[gg * ROWS + r * 8 : gg * ROWS + r * 8 + 8, :] = active_ref[
                0, pl.ds(gg * 2 + r, 8, stride=16), :
            ].astype(F32)

    mine = lax.broadcasted_iota(jnp.int32, (8, 1), 0) == z
    first_half = (1 - x_hi).astype(F32)

    def goal_rows(target, tile, count, factor):
        pair = goals_ref[target, :, cols(tile, count)].astype(F32) * factor
        zero = jnp.zeros((8, count * LANES), F32)
        return jnp.concatenate([jnp.where(mine, pair[r : r + 1], zero) for r in range(2)], axis=0)

    one = jnp.float32(1.0)
    t_a, t_b = 5 * x_hi + core, 2 + 2 * core
    for q in range(NQ):
        for zz in range(3):
            goal_block[q, zz] = goal_rows(t_a, 9 * zz + 3 * q, 3, one)
            goal_block[q, zz + 5] = goal_rows(t_b, 9 * (zz + 5) + 3 * q - 44, 3, first_half)
        goal_block[q, MID] = goal_rows(3, core * 14 + 3 * q, 3, first_half)
        if q == 0:
            goal_block[q, MID + 1] = goal_rows(3, core * 14 + 9, 3, first_half)
        else:
            goal_block[q, MID + 1] = jnp.zeros((ROWS, WIDE), F32)
            if q == 1:
                goal_block[q, MID + 1, :, 0 : 2 * LANES] = goal_rows(3, core * 14 + 12, 2, first_half)
            else:
                goal_block[q, MID + 1, :, 0:LANES] = goal_rows(t_a, 27, 1, one)
                goal_block[q, MID + 1, :, LANES : 2 * LANES] = goal_rows(t_b, 0, 1, first_half)

    wait(xz.at[pl.ds(0, 7)], xz_recv)
    for zz in range(NZ):
        xwide[zz * XROWS : (zz + 1) * XROWS, :] = xz[zz].astype(F32)
    for c in range(TILES):
        xb[g, :, c * LANES : (c + 1) * LANES] = jnp.concatenate(
            [xwide[pl.ds(2 * c + r, 8, stride=XROWS), :] for r in range(2)], axis=0
        ).astype(BF16)

    @pl.loop(1, 8)
    def _(d):
        send(xb.at[g], xb.at[g], xp_send, xp_recv, g_peer(d))

    enc_copy.wait()
    dec_copy.wait()
    wait(xb.at[pl.ds(0, 7)], xp_recv)

    pre = jnp.dot(xb[...].reshape(TOK, D), enc[...], preferred_element_type=F32)
    act = mask[...] * pre
    lat_ref[...] = act.astype(BF16)
    latt_ref[...] = act.T.astype(BF16)

    def decoded(k, tile, count=3):
        return jnp.dot(lat_ref[...], dec[k, :, cols(tile, count)], preferred_element_type=F32)

    def blocks(value):
        return value.reshape(NG, ROWS, value.shape[-1])

    zeros = jnp.zeros((NG, ROWS, LANES), BF16)
    other = (1 - core) * 14
    own = core * 14
    is_a, is_b = send_a.astype(F32), (1 - send_a).astype(F32)

    for q in range(NQ):

        @pl.loop(0, 3)
        def _(i):
            sib_out[q, i] = blocks(decoded(k_s, tile_of(z_s + i, q, send_a)).astype(BF16))

        sib_out[q, 3] = blocks(decoded(k_c, other + 3 * q).astype(BF16))
        if q == 0:
            sib_out[q, 4] = blocks(decoded(k_c, other + 9).astype(BF16))
        elif q == 1:
            sib_out[q, 4, :, :, 0 : 2 * LANES] = blocks(decoded(k_c, other + 12, 2).astype(BF16))
            sib_out[q, 4, :, :, 2 * LANES :] = zeros
        else:
            sib_out[q, 4, :, :, 0:LANES] = blocks((decoded(k_s, 27, 1) * is_a).astype(BF16))
            sib_out[q, 4, :, :, LANES : 2 * LANES] = blocks((decoded(k_s, 0, 1) * is_b).astype(BF16))
            sib_out[q, 4, :, :, 2 * LANES :] = zeros
        send(sib_out.at[q], sib_in.at[q], sib_send.at[q], sib_recv.at[q], sibling)

    for q in range(NQ):

        @pl.loop(0, 3)
        def _(i):
            part[q, :, z_n + i] = blocks(decoded(k_n, tile_of(z_n + i, q, 1 - recv_a)).astype(BF16))

        wait(sib_in.at[q], sib_recv.at[q])

        @pl.loop(0, 3)
        def _(i):
            part[q, :, z_r + i] = (
                blocks(decoded(k_r, tile_of(z_r + i, q, recv_a))) + sib_in[q, i].astype(F32)
            ).astype(BF16)

        part[q, :, MID] = (blocks(decoded(k_c, own + 3 * q)) + sib_in[q, 3].astype(F32)).astype(BF16)

        def last(lanes, value):
            part[q, :, MID + 1, :, lanes] = (
                blocks(value) + sib_in[q, 4, :, :, lanes].astype(F32)
            ).astype(BF16)

        if q == 0:
            last(slice(0, WIDE), decoded(k_c, own + 9))
        elif q == 1:
            last(slice(0, 2 * LANES), decoded(k_c, own + 12, 2))
            part[q, :, MID + 1, :, 2 * LANES :] = zeros
        else:
            last(slice(0, LANES), decoded(k_a, 27, 1))
            last(slice(LANES, 2 * LANES), decoded(k_b, 0, 1))
            part[q, :, MID + 1, :, 2 * LANES :] = zeros

        @pl.loop(1, 8)
        def _(d):
            send(part.at[q, (g + d) % NG], part_in.at[q, d - 1], part_send.at[q], part_recv.at[q], g_peer(d))

    for c in range(TILES):
        block = xb[:, :, c * LANES : (c + 1) * LANES].reshape(TOK, LANES)
        xt[c * LANES : (c + 1) * LANES, :] = block.T

    def plane_sum(q):
        wait(part_in.at[q], part_recv.at[q])

        @pl.loop(0, NZ)
        def _(zz):
            total = part[q, g, zz].astype(F32) - goal_block[q, zz]
            for d in range(7):
                total = total + part_in[q, d, zz].astype(F32)
            zpart[q, zz] = total.astype(BF16)

        @pl.loop(1, 8)
        def _(d):
            send(zpart.at[q, (z + d) % NZ], zpart_in.at[q, d - 1], zp_send.at[q], zp_recv.at[q], z_peer(d))

    def z_sum(q):
        wait(zpart_in.at[q], zp_recv.at[q])
        total = zpart[q, z].astype(F32)
        for d in range(7):
            total = total + zpart_in[q, d].astype(F32)
        xsum[q] = total
        send(xsum.at[q], xsum_in.at[q], xs_send.at[q], xs_recv.at[q], across)

    def x_sum(q):
        wait(xsum_in.at[q], xs_recv.at[q])
        shared = z >= 3
        if q == 2:
            lane = lax.broadcasted_iota(jnp.int32, (ROWS, WIDE), 1)
            private = jnp.logical_or(z < 3, jnp.logical_and(z == 4, lane < LANES))
            shared = jnp.logical_not(private)
        total = xsum[q] + jnp.where(shared, xsum_in[q], 0.0)
        err[q, g, z] = (total * scale).astype(BF16)

        @pl.loop(1, 8)
        def _(d):
            send(err.at[q, g, z], err.at[q, g, z], ez_send.at[q], ez_recv.at[q], z_peer(d))

    def z_spread(q):
        wait(err.at[q, g, pl.ds(0, 7)], ez_recv.at[q])

        @pl.loop(1, 8)
        def _(d):
            send(err.at[q, g], err.at[q, g], ep_send.at[q], ep_recv.at[q], g_peer(d))

    plane_sum(0)
    z_sum(0)
    plane_sum(1)
    x_sum(0)
    z_sum(1)
    plane_sum(2)
    z_spread(0)
    x_sum(1)
    z_sum(2)
    z_spread(1)
    x_sum(2)
    z_spread(2)

    dlat_ref[...] = jnp.zeros_like(dlat_ref)

    def backward(error, k, tile, count=3):
        where = cols(tile, count)
        dlat_ref[...] += lax.dot_general(
            error, dec[k, :, where], (((1,), (1,)), ((), ())), preferred_element_type=F32
        )
        gdec[k, :, where] = jnp.dot(latt_ref[...], error, preferred_element_type=F32).astype(BF16)

    def whole(value):
        return value.reshape(TOK, value.shape[-1])

    for q in range(NQ):
        wait(err.at[q, pl.ds(0, 7)], ep_recv.at[q])
        send(err.at[q, :, pl.ds(z_r, 3)], err_sib.at[q, :, pl.ds(0, 3)], es_send.at[q], es_recv.at[q], sibling)
        send(err.at[q, :, pl.ds(3, 2)], err_sib.at[q, :, pl.ds(3, 2)], es_send.at[q], es_recv.at[q], sibling)

        @pl.loop(0, 3)
        def _(i):
            backward(whole(err[q, :, i]), k_a, tile_of(i, q, 1))
            backward(whole(err[q, :, 5 + i]), k_b, tile_of(5 + i, q, 0))

        backward(whole(err[q, :, MID]), k_c, own + 3 * q)
        if q == 0:
            backward(whole(err[q, :, MID + 1]), k_c, own + 9)
        elif q == 1:
            backward(whole(err[q, :, MID + 1, :, 0 : 2 * LANES]), k_c, own + 12, 2)
        else:
            backward(whole(err[q, :, MID + 1, :, 0:LANES]), k_a, 27, 1)
            backward(whole(err[q, :, MID + 1, :, LANES : 2 * LANES]), k_b, 0, 1)

    for q in range(NQ):
        wait(err_sib.at[q], es_recv.at[q])

        @pl.loop(0, 3)
        def _(i):
            backward(whole(err_sib[q, :, i]), k_s, tile_of(z_s + i, q, send_a))

        backward(whole(err_sib[q, :, 3]), k_c, other + 3 * q)
        if q == 0:
            backward(whole(err_sib[q, :, 4]), k_c, other + 9)
        elif q == 1:
            backward(whole(err_sib[q, :, 4, :, 0 : 2 * LANES]), k_c, other + 12, 2)
        else:
            lanes = pl.ds(pl.multiple_of((1 - send_a) * LANES, LANES), LANES)
            backward(whole(err_sib[q, :, 4, :, lanes]), k_s, 27 * send_a, 1)

    gdec_copy = pltpu.make_async_copy(gdec, gdec_hbm.at[0], out_sem.at[0])
    gdec_copy.start()
    dpre = (mask[...] * dlat_ref[...]).astype(BF16)
    genc[...] = jnp.dot(xt[...], dpre, preferred_element_type=F32).astype(BF16)
    genc_copy = pltpu.make_async_copy(genc, genc_hbm.at[0], out_sem.at[1])
    genc_copy.start()

    wait(xz.at[pl.ds(0, 7)], xz_send)
    wait(xb.at[pl.ds(0, 7)], xp_send)
    for q in range(NQ):
        wait(sib_in.at[q], sib_send.at[q])
        wait(part_in.at[q], part_send.at[q])
        wait(zpart_in.at[q], zp_send.at[q])
        wait(xsum_in.at[q], xs_send.at[q])
        wait(zpart_in.at[q], ez_send.at[q])
        wait(err.at[q, pl.ds(0, 7)], ep_send.at[q])
        wait(err_sib.at[q], es_send.at[q])
    gdec_copy.wait()
    genc_copy.wait()


def local(inputs, encoder, active, decoder, goals):
    vmem = pl.BlockSpec(memory_space=pltpu.VMEM)
    hbm = pl.BlockSpec(memory_space=pl.ANY)
    dma = pltpu.SemaphoreType.DMA
    per_q = [dma((NQ,))] * 2
    return pl.pallas_call(
        kernel,
        out_shape=(
            jax.ShapeDtypeStruct((1, D, FL), BF16),
            jax.ShapeDtypeStruct((1, 4, FL, D), BF16),
        ),
        in_specs=[vmem, vmem, vmem, hbm, hbm],
        out_specs=(hbm, hbm),
        scratch_shapes=[
            pltpu.VMEM((D, FL), BF16),
            pltpu.VMEM((4, FL, D), BF16),
            pltpu.VMEM((4, FL, D), BF16),
            pltpu.VMEM((D, FL), BF16),
            pltpu.VMEM((XROWS, LANES), F32),
            pltpu.VMEM((NZ, XROWS, LANES), BF16),
            pltpu.VMEM((NZ * XROWS, LANES), F32),
            pltpu.VMEM((NG, ROWS, D), BF16),
            pltpu.VMEM((D, TOK), BF16),
            pltpu.VMEM((TOK, FL), F32),
            pltpu.VMEM((TOK, FL), BF16),
            pltpu.VMEM((FL, TOK), BF16),
            pltpu.VMEM((TOK, FL), F32),
            pltpu.VMEM((NQ, NZ, ROWS, WIDE), F32),
            pltpu.VMEM((NQ, 5, NG, ROWS, WIDE), BF16),
            pltpu.VMEM((NQ, 5, NG, ROWS, WIDE), BF16),
            pltpu.VMEM((NQ, NG, NZ, ROWS, WIDE), BF16),
            pltpu.VMEM((NQ, NG - 1, NZ, ROWS, WIDE), BF16),
            pltpu.VMEM((NQ, NZ, ROWS, WIDE), BF16),
            pltpu.VMEM((NQ, NZ - 1, ROWS, WIDE), BF16),
            pltpu.VMEM((NQ, ROWS, WIDE), F32),
            pltpu.VMEM((NQ, ROWS, WIDE), F32),
            pltpu.VMEM((NQ, NG, NZ, ROWS, WIDE), BF16),
            pltpu.VMEM((NQ, NG, 5, ROWS, WIDE), BF16),
            dma((2,)),
            dma((2,)),
            dma,
            dma,
            dma,
            dma,
            *per_q,
            *per_q,
            *per_q,
            *per_q,
            *per_q,
            *per_q,
            *per_q,
        ],
        compiler_params=pltpu.CompilerParams(
            collective_id=0, has_side_effects=True, vmem_limit_bytes=56 * 2**20
        ),
        name="step",
    )(inputs, goals, active, encoder, decoder)


def solution(mesh):
    return jax.shard_map(
        local,
        mesh=mesh,
        in_specs=(
            P("layer", "slab", None),
            P("layer", None, "slab"),
            P("layer", None, "slab"),
            P("layer", None, "slab", None),
            P(None, "slab", None),
        ),
        out_specs=(P("layer", None, "slab"), P("layer", None, "slab", None)),
        check_vma=False,
    )
```

time: 1170 us -> 106 us (0.09)
  the two profiles are of different devices: /device:TPU:8 before, /device:TPU:1 now
where the time goes in v1:
time: 106 us
  Pallas kernels  98.9 us (93%)
  local copies, waits for them, and re-layouts  6.27 us (6%)
    pallas_call x1, Pallas kernels, local(): pl.pallas_call(kernel, out_shape=(jax.ShapeDtypeStruct((1, D, FL), BF16),...  98.9 us
    unnamed x2, local copies, waits for them, and re-layouts  6.27 us

profile of v1, /device:TPU:1, one launch (start us, length us, event | category | flops | bytes accessed | tf_op | source)
XLA Modules:
  0.0 105.8 jit_solution(2465861656104853551)
XLA Ops:
  0.6 98.9 %step.1 = (bf16[1,3584,128]{2,1,0:T(8,128)(2,1)}, bf16[1,4,128,3584]{3,2,1,0:T(8,128)(2,1)}) custom-call(bf16[1,2,3584]{2,1,0:T(2,128)(2,1)} %inputs_ref.1, bf16[7,2,3584]{2,1,0:T(2,128)(2,1)} %goals_ref.1, s32[1,128,128]{2,1,0:T(8,128)} %active_ref.1, bf16[1,3584,128]{2,1,0:T(8,128)(2,1)} %enc_hbm.1, bf16[1,4,128,3584]{3,2,1,0:T(8,128)(2,1)} %dec_hbm.1), custom_call_target="tpu_custom_call" | custom-call | tf_op jit(solution)/shard_map/step/pallas_call | solution.py:392
  99.5 2.2 %copy.9 = bf16[1,3584,128]{2,1,0:T(8,128)(2,1)} copy(bf16[1,3584,128]{2,1,0:T(8,128)(2,1)} %get-tuple-element.4) | data formatting | bytes 1835008
  101.7 4.1 %copy.10 = bf16[1,4,128,3584]{3,2,1,0:T(8,128)(2,1)} copy(bf16[1,4,128,3584]{3,2,1,0:T(8,128)(2,1)} %get-tuple-element.5) | data formatting | bytes 7340032

commit v2 on v1

v2 whole, which is shorter than its diff:
```python
import math

import jax
import jax.numpy as jnp
from jax import lax
from jax.experimental import pallas as pl
from jax.experimental.pallas import tpu as pltpu
from jax.sharding import PartitionSpec as P

MESH = pl.DeviceIdType.MESH
F32, BF16 = jnp.float32, jnp.bfloat16

NZ, NG = 8, 8
TOK, D, FL = 128, 3584, 128
ROWS = 16
LANES = 128
TILES = D // LANES
NQ = 3
WIDE = 3 * LANES
XROWS = 64
MID = 3
FAR_FIRST = (4, 3, 5, 2, 6, 1, 7, 0)


def cols(tile, count=3):
    return pl.ds(pl.multiple_of(tile * LANES, LANES), count * LANES)


def kernel(
    inputs_hbm,
    goals_hbm,
    active_hbm,
    enc_hbm,
    dec_hbm,
    gdec,
    xt,
    mask,
    dlat_ref,
    inputs_ref,
    goals_ref,
    active_ref,
    enc,
    dec,
    xstage,
    xz,
    xwide,
    xb,
    lat_ref,
    latt_ref,
    goal_block,
    sib_out,
    sib_in,
    part,
    y_in,
    z_in,
    err,
    err_far,
    err_sib,
    load_sem,
    xz_send,
    xz_recv,
    xb_send,
    xb_recv,
    sib_send,
    sib_recv,
    y_send,
    y_recv,
    z_send,
    z_recv,
    ez_send,
    ez_recv,
    ef_send,
    ef_recv,
    ep_send,
    ep_recv,
    es_send,
    es_recv,
):
    layer = lax.axis_index("layer")
    slab = lax.axis_index("slab")
    x_hi, core = layer // 2, layer % 2
    z, g = slab // NG, slab % NG
    y, x = g // 2, g % 2
    y1, y2, y3 = (y + 1) % 4, (y + 2) % 4, (y + 3) % 4
    keep = (x + x_hi) % 2
    g_keep, g_pass = y * 2 + keep, y * 2 + 1 - keep
    scale = 1.0 / math.sqrt(TOK)

    def z_peer(d):
        return (layer, ((z + d) % NZ) * NG + g)

    def pair_z(d):
        return (layer, ((z + d) % NZ) * NG + y * 2 + 1 - x)

    def across_z(d):
        return ((1 - x_hi) * 2 + core, ((z + d) % NZ) * NG + y * 2 + 1 - x)

    right = (layer, z * NG + y1 * 2 + x)
    left = (layer, z * NG + y3 * 2 + x)
    pair = (layer, z * NG + y * 2 + 1 - x)
    sibling = (x_hi * 2 + 1 - core, slab)
    right_pair = (layer, z * NG + y1 * 2 + 1 - x)
    left_pair = (layer, z * NG + y3 * 2 + 1 - x)

    k_a = 3 * x_hi
    k_b = (layer + 2) % 4
    k_c = 3 - layer
    k_s = 1 + x_hi
    send_a = (core + x_hi + 1) % 2
    recv_a = 1 - send_a
    k_r = recv_a * k_a + (1 - recv_a) * k_b
    k_n = (1 - recv_a) * k_a + recv_a * k_b
    z_s, z_r, z_n = 5 * (1 - send_a), 5 * (1 - recv_a), 5 * recv_a

    def first_tile(q, is_a):
        return 9 * q + 1 - is_a

    loads = [
        pltpu.make_async_copy(src, dst, load_sem.at[i])
        for i, (src, dst) in enumerate(
            [
                (inputs_hbm.at[0], inputs_ref),
                (active_hbm.at[0], active_ref),
                (goals_hbm, goals_ref),
                (enc_hbm.at[0], enc),
                (dec_hbm.at[0], dec),
            ]
        )
    ]
    for load in loads:
        load.start()

    barrier = pltpu.get_barrier_semaphore()

    def greet(device):
        pl.semaphore_signal(barrier, inc=1, device_id=device, device_id_type=MESH)

    for d in FAR_FIRST:
        greet(across_z(d))
        greet(pair_z(d))
        if d:
            greet(z_peer(d))
    for device in (right, left, right_pair, left_pair, sibling):
        greet(device)

    xstage[...] = jnp.zeros_like(xstage)
    loads[0].wait()
    for c in range(TILES):
        xstage[2 * c : 2 * c + 2, :] = inputs_ref[:, c * LANES : (c + 1) * LANES].astype(F32)
    xz[z] = xstage[...].astype(BF16)

    pl.semaphore_wait(barrier, 28)

    def send(src, dst, ssem, rsem, device):
        pltpu.make_async_remote_copy(
            src_ref=src, dst_ref=dst, send_sem=ssem, recv_sem=rsem, device_id=device, device_id_type=MESH
        ).start()

    def wait(ref, sem):
        pltpu.make_async_copy(ref, ref, sem).wait()

    class Spread:
        def __init__(self, buf, half, near, mate, ssem, rsem):
            self.buf, self.half, self.near, self.mate = buf, half, near, mate
            self.ssem, self.rsem = ssem, rsem

        def put(self, block, slot, device):
            send(self.buf.at[block], self.buf.at[block], self.ssem, self.rsem(slot), device)

        def put_half(self, block, i, slot, device):
            part_of = self.half(block, i)
            send(part_of, part_of, self.ssem, self.rsem(slot), device)

        def got(self, slot):
            wait(self.buf.at[0], self.rsem(slot))

        def start(self):
            own = y * 2 + self.near
            self.put(own, 1, right)
            self.put(own, 2, left)
            self.put(own, 3, right_pair)
            self.put(own, 4, left_pair)
            self.put(own, 0, pair)

        def onward(self, which, slot):
            self.got(slot)
            self.put_half(y3 * 2 + which, 0, slot + 4, right)
            self.got(slot + 1)
            self.put_half(y1 * 2 + which, 1, slot + 5, left)

        def second(self):
            self.onward(self.near, 1)

        def third(self):
            self.onward(self.mate, 3)

        def finish(self):
            self.got(0)
            for slot in range(5, 9):
                wait(self.half(0, 0), self.rsem(slot))

        def left_here(self):
            wait(self.buf.at[pl.ds(0, 7)], self.ssem)

    for d in FAR_FIRST[:7]:
        send(xz.at[z], xz.at[z], xz_send, xz_recv, z_peer(d))

    loads[1].wait()
    for gg in range(NG):
        for r in range(2):
            mask[gg * ROWS + r * 8 : gg * ROWS + r * 8 + 8, :] = active_ref[
                pl.ds(gg * 2 + r, 8, stride=16), :
            ].astype(F32)

    mine = lax.broadcasted_iota(jnp.int32, (8, 1), 0) == z
    loads[2].wait()

    first_half = (1 - x_hi).astype(F32)

    def goal_rows(target, tile, count, factor=first_half):
        two = goals_ref[target, :, cols(tile, count)].astype(F32) * factor
        zero = jnp.zeros((8, count * LANES), F32)
        return jnp.concatenate([jnp.where(mine, two[r : r + 1], zero) for r in range(2)], axis=0)

    t_a, t_b = 5 * x_hi + core, 2 + 2 * core
    for q in range(NQ):
        for zz in range(3):
            goal_block[q, zz] = goal_rows(t_a, 9 * q + 3 * zz, 3, 1.0)
            goal_block[q, zz + 5] = goal_rows(t_b, 9 * q + 3 * zz + 1, 3)
        goal_block[q, MID] = goal_rows(3, core * 14 + 3 * q, 3)
        if q == 0:
            goal_block[q, MID + 1] = goal_rows(3, core * 14 + 9, 3)
        else:
            goal_block[q, MID + 1] = jnp.zeros((ROWS, WIDE), F32)
            if q == 1:
                goal_block[q, MID + 1, :, 0 : 2 * LANES] = goal_rows(3, core * 14 + 12, 2)
            else:
                goal_block[q, MID + 1, :, 0:LANES] = goal_rows(t_a, 27, 1, 1.0)
                goal_block[q, MID + 1, :, LANES : 2 * LANES] = goal_rows(t_b, 0, 1)

    wait(xz.at[pl.ds(0, 7)], xz_recv)
    for zz in range(NZ):
        xwide[zz * XROWS : (zz + 1) * XROWS, :] = xz[zz].astype(F32)
    for c in range(TILES):
        xb[g, c // 14, :, (c % 14) * LANES : (c % 14 + 1) * LANES] = jnp.concatenate(
            [xwide[pl.ds(2 * c + r, 8, stride=XROWS), :] for r in range(2)], axis=0
        ).astype(BF16)

    x_spread = Spread(xb, lambda b, i: xb.at[b, i], x, 1 - x, xb_send, lambda slot: xb_recv.at[slot])
    x_spread.start()
    x_spread.second()
    x_spread.third()
    loads[3].wait()
    loads[4].wait()
    x_spread.finish()

    pre = jnp.dot(xb[:, 0].reshape(TOK, D // 2), enc[: D // 2, :], preferred_element_type=F32)
    pre = pre + jnp.dot(xb[:, 1].reshape(TOK, D // 2), enc[D // 2 :, :], preferred_element_type=F32)
    act = mask[...] * pre
    lat_ref[...] = act.astype(BF16)
    latt_ref[...] = act.T.astype(BF16)

    def decoded(k, tile, count=3):
        return jnp.dot(lat_ref[...], dec[k, :, cols(tile, count)], preferred_element_type=F32)

    def blocks(value):
        return value.reshape(NG, ROWS, value.shape[-1])

    zeros = jnp.zeros((NG, ROWS, LANES), BF16)
    other = (1 - core) * 14
    own = core * 14
    is_a, is_b = send_a.astype(F32), (1 - send_a).astype(F32)

    def for_sibling(q):
        wide = decoded(k_s, first_tile(q, send_a), 9).astype(BF16)
        for i in range(3):
            sib_out[q, i] = blocks(wide[:, i * WIDE : (i + 1) * WIDE])

        sib_out[q, 3] = blocks(decoded(k_c, other + 3 * q).astype(BF16))
        if q == 0:
            sib_out[q, 4] = blocks(decoded(k_c, other + 9).astype(BF16))
        elif q == 1:
            sib_out[q, 4, :, :, 0 : 2 * LANES] = blocks(decoded(k_c, other + 12, 2).astype(BF16))
            sib_out[q, 4, :, :, 2 * LANES :] = zeros
        else:
            sib_out[q, 4, :, :, 0:LANES] = blocks((decoded(k_s, 27, 1) * is_a).astype(BF16))
            sib_out[q, 4, :, :, LANES : 2 * LANES] = blocks((decoded(k_s, 0, 1) * is_b).astype(BF16))
            sib_out[q, 4, :, :, 2 * LANES :] = zeros
        send(sib_out.at[q], sib_in.at[q], sib_send.at[q], sib_recv.at[q], sibling)

    def own_alone(q):
        wide = decoded(k_n, first_tile(q, 1 - recv_a), 9).astype(BF16)
        for i in range(3):
            part[q, :, z_n + i] = blocks(wide[:, i * WIDE : (i + 1) * WIDE])

    def own_shared(q):
        wait(sib_in.at[q], sib_recv.at[q])

        wide = decoded(k_r, first_tile(q, recv_a), 9)
        for i in range(3):
            part[q, :, z_r + i] = (
                blocks(wide[:, i * WIDE : (i + 1) * WIDE]) + sib_in[q, i].astype(F32)
            ).astype(BF16)

        part[q, :, MID] = (blocks(decoded(k_c, own + 3 * q)) + sib_in[q, 3].astype(F32)).astype(BF16)

        def last(lanes, value):
            part[q, :, MID + 1, :, lanes] = (
                blocks(value) + sib_in[q, 4, :, :, lanes].astype(F32)
            ).astype(BF16)

        if q == 0:
            last(slice(0, WIDE), decoded(k_c, own + 9))
        elif q == 1:
            last(slice(0, 2 * LANES), decoded(k_c, own + 12, 2))
            part[q, :, MID + 1, :, 2 * LANES :] = zeros
        else:
            last(slice(0, LANES), decoded(k_a, 27, 1))
            last(slice(LANES, 2 * LANES), decoded(k_b, 0, 1))
            part[q, :, MID + 1, :, 2 * LANES :] = zeros

    def y_first(q):
        ss = y_send.at[q]
        send(part.at[q, y2 * 2], y_in.at[q, 0], ss, y_recv.at[q, 0], right)
        send(part.at[q, y2 * 2 + 1], y_in.at[q, 1], ss, y_recv.at[q, 1], left)
        send(part.at[q, y1 * 2 + 1], y_in.at[q, 2], ss, y_recv.at[q, 2], right)
        send(part.at[q, y3 * 2], y_in.at[q, 3], ss, y_recv.at[q, 2], left)

    def y_second(q):
        ss = y_send.at[q]
        wait(y_in.at[q, 0], y_recv.at[q, 0])
        for zz in range(NZ):
            part[q, y1 * 2, zz] = (part[q, y1 * 2, zz].astype(F32) + y_in[q, 0, zz].astype(F32)).astype(BF16)
        send(part.at[q, y1 * 2], y_in.at[q, 4], ss, y_recv.at[q, 2], right)
        wait(y_in.at[q, 1], y_recv.at[q, 1])
        for zz in range(NZ):
            part[q, y3 * 2 + 1, zz] = (
                part[q, y3 * 2 + 1, zz].astype(F32) + y_in[q, 1, zz].astype(F32)
            ).astype(BF16)
        send(part.at[q, y3 * 2 + 1], y_in.at[q, 5], ss, y_recv.at[q, 2], left)

    def y_sum(q):
        wait(y_in.at[q, pl.ds(0, 4)], y_recv.at[q, 2])
        for half, (one, two) in enumerate(((3, 4), (2, 5))):
            here = (x == half).astype(F32)
            for zz in range(NZ):
                part[q, y * 2 + half, zz] = (
                    part[q, y * 2 + half, zz].astype(F32)
                    + y_in[q, one, zz].astype(F32)
                    + y_in[q, two, zz].astype(F32)
                    - goal_block[q, zz] * here
                ).astype(BF16)
        for d in FAR_FIRST:
            zd = (z + d) % NZ
            send(part.at[q, g_pass, zd], z_in.at[q, 7 + d], z_send.at[q], z_recv.at[q], pair_z(d))
            if d:
                send(part.at[q, g_keep, zd], z_in.at[q, d - 1], z_send.at[q], z_recv.at[q], z_peer(d))

    def z_sum(q):
        wait(z_in.at[q], z_recv.at[q])
        total = part[q, g_keep, z].astype(F32)
        for i in range(15):
            total = total + z_in[q, i].astype(F32)
        err[q, g_keep, z] = (total * scale).astype(BF16)
        own = err.at[q, g_keep, z]
        for d in FAR_FIRST[:7]:
            send(own, own, ez_send.at[q], ez_recv.at[q], z_peer(d))

        @pl.when(z >= 3)
        def _():
            for d in FAR_FIRST:
                send(own, err_far.at[q, z - 3], ef_send.at[q], ef_recv.at[q], across_z(d))

    spreads = [
        Spread(
            err.at[q],
            lambda b, i, q=q: err.at[q, b, pl.ds(4 * i, 4)],
            keep,
            1 - keep,
            ep_send.at[q],
            lambda slot, q=q: ep_recv.at[q, slot],
        )
        for q in range(NQ)
    ]

    def z_spread(q):
        wait(err.at[q, 0, pl.ds(0, 7)], ez_recv.at[q])
        wait(err_far.at[q], ef_recv.at[q])
        wait(err.at[q, 0, pl.ds(0, 7)], ez_send.at[q])

        @pl.when(z >= 3)
        def _():
            wait(err.at[q, 0], ef_send.at[q])

        for zz in range(3, NZ):
            far = err_far[q, zz - 3].astype(F32)
            if q == 2 and zz == 4:
                lane = lax.broadcasted_iota(jnp.int32, (ROWS, WIDE), 1)
                far = jnp.where(lane < LANES, 0.0, far)
            err[q, g_keep, zz] = (err[q, g_keep, zz].astype(F32) + far).astype(BF16)
        spreads[q].start()

    def arrived(q):
        spreads[q].finish()
        send(err.at[q, :, pl.ds(z_r, 3)], err_sib.at[q, :, pl.ds(0, 3)], es_send.at[q], es_recv.at[q], sibling)
        send(err.at[q, :, pl.ds(3, 2)], err_sib.at[q, :, pl.ds(3, 2)], es_send.at[q], es_recv.at[q], sibling)

    def backward(error, k, tile, count=3):
        where = cols(tile, count)
        dlat_ref[...] += lax.dot_general(
            error, dec[k, :, where], (((1,), (1,)), ((), ())), preferred_element_type=F32
        )
        gdec[k, :, where] = jnp.dot(latt_ref[...], error, preferred_element_type=F32).astype(BF16)

    def whole(value):
        return value.reshape(TOK, value.shape[-1])

    def wide(ref, q, at):
        return jnp.concatenate([whole(ref[q, :, at + i]) for i in range(3)], axis=1)

    def own_back(q):
        backward(wide(err, q, 0), k_a, first_tile(q, 1), 9)
        backward(wide(err, q, 5), k_b, first_tile(q, 0), 9)

        backward(whole(err[q, :, MID]), k_c, own + 3 * q)
        if q == 0:
            backward(whole(err[q, :, MID + 1]), k_c, own + 9)
        elif q == 1:
            backward(whole(err[q, :, MID + 1, :, 0 : 2 * LANES]), k_c, own + 12, 2)
        else:
            backward(whole(err[q, :, MID + 1, :, 0:LANES]), k_a, 27, 1)
            backward(whole(err[q, :, MID + 1, :, LANES : 2 * LANES]), k_b, 0, 1)

    def sibling_back(q):
        wait(err_sib.at[q], es_recv.at[q])

        backward(wide(err_sib, q, 0), k_s, first_tile(q, send_a), 9)

        backward(whole(err_sib[q, :, 3]), k_c, other + 3 * q)
        if q == 0:
            backward(whole(err_sib[q, :, 4]), k_c, other + 9)
        elif q == 1:
            backward(whole(err_sib[q, :, 4, :, 0 : 2 * LANES]), k_c, other + 12, 2)
        else:
            lanes = pl.ds(pl.multiple_of((1 - send_a) * LANES, LANES), LANES)
            backward(whole(err_sib[q, :, 4, :, lanes]), k_s, 27 * send_a, 1)

    for_sibling(0)
    own_alone(0)
    for_sibling(1)
    own_shared(0)
    y_first(0)
    own_alone(1)
    for_sibling(2)
    own_shared(1)
    y_first(1)
    own_alone(2)
    y_second(0)
    own_shared(2)
    y_first(2)
    y_second(1)
    y_sum(0)
    y_second(2)
    y_sum(1)
    for c in range(TILES):
        block = xb[:, c // 14, :, (c % 14) * LANES : (c % 14 + 1) * LANES].reshape(TOK, LANES)
        xt[c * LANES : (c + 1) * LANES, :] = block.T
    dlat_ref[...] = jnp.zeros_like(dlat_ref)
    z_sum(0)
    y_sum(2)
    z_sum(1)
    z_spread(0)
    z_sum(2)
    z_spread(1)
    spreads[0].second()
    spreads[0].third()
    z_spread(2)
    spreads[1].second()
    arrived(0)
    spreads[1].third()
    own_back(0)
    spreads[2].second()
    spreads[2].third()
    arrived(1)
    sibling_back(0)
    own_back(1)
    sibling_back(1)
    arrived(2)
    own_back(2)
    sibling_back(2)

    wait(xz.at[pl.ds(0, 7)], xz_send)
    x_spread.left_here()
    for q in range(NQ):
        wait(sib_in.at[q], sib_send.at[q])
        wait(y_in.at[q], y_send.at[q])
        wait(z_in.at[q], z_send.at[q])
        spreads[q].left_here()
        wait(err_sib.at[q], es_send.at[q])


def last_kernel(gdec, xt, mask, dlat, genc_hbm, gdec_hbm, genc, sem):
    gdec_copy = pltpu.make_async_copy(gdec, gdec_hbm.at[0], sem.at[0])
    gdec_copy.start()
    dpre = (mask[...] * dlat[...]).astype(BF16)
    genc[...] = jnp.dot(xt[...], dpre, preferred_element_type=F32).astype(BF16)
    genc_copy = pltpu.make_async_copy(genc, genc_hbm.at[0], sem.at[1])
    genc_copy.start()
    gdec_copy.wait()
    genc_copy.wait()


def local(inputs, encoder, active, decoder, goals):
    vmem = pl.BlockSpec(memory_space=pltpu.VMEM)
    hbm = pl.BlockSpec(memory_space=pl.ANY)
    dma = pltpu.SemaphoreType.DMA
    per_q = [dma((NQ,))] * 2
    gdec, xt, mask, dlat = pl.pallas_call(
        kernel,
        out_shape=(
            pltpu.VMEM((4, FL, D), BF16),
            pltpu.VMEM((D, TOK), BF16),
            pltpu.VMEM((TOK, FL), F32),
            pltpu.VMEM((TOK, FL), F32),
        ),
        in_specs=[pl.BlockSpec(memory_space=pltpu.HBM)] * 5,
        out_specs=[vmem] * 4,
        scratch_shapes=[
            pltpu.VMEM((2, D), BF16),
            pltpu.VMEM((7, 2, D), BF16),
            pltpu.VMEM((TOK, FL), jnp.int32),
            pltpu.VMEM((D, FL), BF16),
            pltpu.VMEM((4, FL, D), BF16),
            pltpu.VMEM((XROWS, LANES), F32),
            pltpu.VMEM((NZ, XROWS, LANES), BF16),
            pltpu.VMEM((NZ * XROWS, LANES), F32),
            pltpu.VMEM((NG, 2, ROWS, D // 2), BF16),
            pltpu.VMEM((TOK, FL), BF16),
            pltpu.VMEM((FL, TOK), BF16),
            pltpu.VMEM((NQ, NZ, ROWS, WIDE), F32),
            pltpu.VMEM((NQ, 5, NG, ROWS, WIDE), BF16),
            pltpu.VMEM((NQ, 5, NG, ROWS, WIDE), BF16),
            pltpu.VMEM((NQ, NG, NZ, ROWS, WIDE), BF16),
            pltpu.VMEM((NQ, 6, NZ, ROWS, WIDE), BF16),
            pltpu.VMEM((NQ, 15, ROWS, WIDE), BF16),
            pltpu.VMEM((NQ, NG, NZ, ROWS, WIDE), BF16),
            pltpu.VMEM((NQ, 5, ROWS, WIDE), BF16),
            pltpu.VMEM((NQ, NG, 5, ROWS, WIDE), BF16),
            dma((5,)),
            dma,
            dma,
            dma,
            dma((9,)),
            *per_q,
            dma((NQ,)),
            dma((NQ, 3)),
            *per_q,
            *per_q,
            *per_q,
            dma((NQ,)),
            dma((NQ, 9)),
            *per_q,
        ],
        compiler_params=pltpu.CompilerParams(
            collective_id=0, has_side_effects=True, vmem_limit_bytes=54 * 2**20
        ),
        name="step",
    )(inputs, goals, active, encoder, decoder)
    return pl.pallas_call(
        last_kernel,
        out_shape=(
            jax.ShapeDtypeStruct((1, D, FL), BF16),
            jax.ShapeDtypeStruct((1, 4, FL, D), BF16),
        ),
        in_specs=[vmem] * 4,
        out_specs=(hbm, hbm),
        scratch_shapes=[pltpu.VMEM((D, FL), BF16), dma((2,))],
        compiler_params=pltpu.CompilerParams(vmem_limit_bytes=8 * 2**20),
        name="write",
    )(gdec, xt, mask, dlat)


def solution(mesh):
    return jax.shard_map(
        local,
        mesh=mesh,
        in_specs=(
            P("layer", "slab", None),
            P("layer", None, "slab"),
            P("layer", None, "slab"),
            P("layer", None, "slab", None),
            P(None, "slab", None),
        ),
        out_specs=(P("layer", None, "slab"), P("layer", None, "slab", None)),
        check_vma=False,
    )
```

time: 106 us -> 91.9 us (0.87)
  Pallas kernels: 98.9 us -> 91.1 us
  local copies, waits for them, and re-layouts: 6.27 us -> 0 us
    pallas_call x1 -> x2, Pallas kernels: 98.9 us -> 91.1 us  [the longest x1 89 us: local(): pl.pallas_call(kernel, out_shape=(pltpu.VMEM((4, FL, D), BF16), pltpu.VME...]
    unnamed x2 -> x0, local copies, waits for them, and re-layouts: 6.27 us -> none
where the time goes in v2:
time: 91.9 us; the launch traced here: 91.8 us
  Pallas kernels  91.1 us (99%)
    pallas_call x1, Pallas kernels, local(): pl.pallas_call(kernel, out_shape=(pltpu.VMEM((4, FL, D), BF16), pltpu.VME...  89 us
    pallas_call x1, Pallas kernels, local(): pl.pallas_call(last_kernel, out_shape=(jax.ShapeDtypeStruct((1, D, FL), B...  2.15 us

profile of v2, /device:TPU:1, one launch (start us, length us, event | category | flops | bytes accessed | tf_op | source)
XLA Modules:
  0.0 91.8 jit_solution(214938493012652863)
XLA Ops:
  0.6 89.0 %step.1 = (bf16[4,128,3584]{2,1,0:T(8,128)(2,1)S(1)}, bf16[3584,128]{1,0:T(8,128)(2,1)S(1)}, f32[128,128]{1,0:T(8,128)S(1)}, f32[128,128]{1,0:T(8,128)S(1)}) custom-call(bf16[1,2,3584]{2,1,0:T(2,128)(2,1)} %inputs_hbm.1, bf16[7,2,3584]{2,1,0:T(2,128)(2,1)} %goals_hbm.1, s32[1,128,128]{2,1,0:T(8,128)} %active_hbm.1, bf16[1,3584,128]{2,1,0:T(8,128)(2,1)} %enc_hbm.1, ...), custom_call_target="tpu_custom_call" | custom-call | tf_op jit(solution)/shard_map/step/pallas_call | solution.py:518
  89.6 2.1 %write.1 = (bf16[1,3584,128]{2,1,0:T(8,128)(2,1)}, bf16[1,4,128,3584]{3,2,1,0:T(8,128)(2,1)}) custom-call(bf16[4,128,3584]{2,1,0:T(8,128)(2,1)S(1)} %get-tuple-element.6.gdec, bf16[3584,128]{1,0:T(8,128)(2,1)S(1)} %get-tuple-element.7.xt, f32[128,128]{1,0:T(8,128)S(1)} %get-tuple-element.8.mask, f32[128,128]{1,0:T(8,128)S(1)} %get-tuple-element.9.dlat), custom_call_target="tpu_custom_call" | custom-call | tf_op jit(solution)/shard_map/write/pallas_call | solution.py:569

commit v3 on v2

v3 whole, which is shorter than its diff:
```python
import math

import jax
import jax.numpy as jnp
from jax import lax
from jax.experimental import pallas as pl
from jax.experimental.pallas import tpu as pltpu
from jax.sharding import PartitionSpec as P

MESH = pl.DeviceIdType.MESH
F32, BF16 = jnp.float32, jnp.bfloat16

NZ, NG = 8, 8
TOK, D, FL = 128, 3584, 128
ROWS = 16
LANES = 128
TILES = D // LANES
NQ = 3
TILES_OF = (4, 3, 2)
FIRST = (0, 4, 7)
XROWS = 64
MID = 3
FAR_FIRST = (4, 3, 5, 2, 6, 1, 7, 0)


def cols(tile, count=3):
    return pl.ds(pl.multiple_of(tile * LANES, LANES), count * LANES)


def kernel(
    inputs_hbm,
    goals_hbm,
    active_hbm,
    enc_hbm,
    dec_hbm,
    gdec,
    xt,
    mask,
    dlat_ref,
    inputs_ref,
    goals_ref,
    active_ref,
    enc,
    dec,
    xstage,
    xz,
    xwide,
    xb,
    lat_ref,
    latt_ref,
    goal_block,
    sib_out,
    sib_in,
    part,
    y_in,
    half_in,
    pair_in,
    x_in,
    z_in,
    bulk_in,
    plane_in,
    term,
    err,
    err_far,
    plane_far,
    err_sib,
    load_sem,
    xz_send,
    xz_recv,
    xb_send,
    xb_recv,
    sib_send,
    sib_recv,
    y_send,
    y_recv,
    x_send,
    x_recv,
    pair_recv,
    z_send,
    z_recv,
    ez_send,
    ez_recv,
    ef_send,
    ef_recv,
    ep_send,
    ep_recv,
    es_send,
    es_recv,
    bulk_send,
    bulk_recv,
    plane_send,
    plane_recv,
    far_send,
    far_recv,
):
    layer = lax.axis_index("layer")
    slab = lax.axis_index("slab")
    x_hi, core = layer // 2, layer % 2
    z, g = slab // NG, slab % NG
    y, x = g // 2, g % 2
    y1, y2, y3 = (y + 1) % 4, (y + 2) % 4, (y + 3) % 4
    keep = (x + x_hi) % 2
    g_keep, g_pass = y * 2 + keep, y * 2 + 1 - keep
    scale = 1.0 / math.sqrt(TOK)

    def z_peer(d):
        return (layer, ((z + d) % NZ) * NG + g)

    def plane_peer(d):
        return (layer, z * NG + (g + d) % NG)

    def across_plane(d):
        return ((1 - x_hi) * 2 + core, z * NG + (g + d) % NG)

    def across_z(d):
        return ((1 - x_hi) * 2 + core, ((z + d) % NZ) * NG + y * 2 + 1 - x)

    right = (layer, z * NG + y1 * 2 + x)
    left = (layer, z * NG + y3 * 2 + x)
    pair = (layer, z * NG + y * 2 + 1 - x)
    sibling = (x_hi * 2 + 1 - core, slab)
    right_pair = (layer, z * NG + y1 * 2 + 1 - x)
    left_pair = (layer, z * NG + y3 * 2 + 1 - x)

    k_a = 3 * x_hi
    k_b = (layer + 2) % 4
    k_c = 3 - layer
    k_s = 1 + x_hi
    send_a = (core + x_hi + 1) % 2
    recv_a = 1 - send_a
    k_r = recv_a * k_a + (1 - recv_a) * k_b
    k_n = (1 - recv_a) * k_a + recv_a * k_b
    z_s, z_r, z_n = 5 * (1 - send_a), 5 * (1 - recv_a), 5 * recv_a

    def first_tile(q, is_a):
        return 3 * FIRST[q] + 1 - is_a

    loads = [
        pltpu.make_async_copy(src, dst, load_sem.at[i])
        for i, (src, dst) in enumerate(
            [
                (inputs_hbm.at[0], inputs_ref),
                (active_hbm.at[0], active_ref),
                (goals_hbm, goals_ref),
                (enc_hbm.at[0], enc),
                (dec_hbm.at[0], dec),
            ]
        )
    ]
    for load in loads:
        load.start()

    barrier = pltpu.get_barrier_semaphore()

    def greet(device):
        pl.semaphore_signal(barrier, inc=1, device_id=device, device_id_type=MESH)

    for d in FAR_FIRST:
        greet(across_z(d))
        greet(across_plane(d))
        if d:
            greet(z_peer(d))
            greet(plane_peer(d))
    greet(sibling)

    xstage[...] = jnp.zeros_like(xstage)
    loads[0].wait()
    for c in range(TILES):
        xstage[2 * c : 2 * c + 2, :] = inputs_ref[:, c * LANES : (c + 1) * LANES].astype(F32)
    xz[z] = xstage[...].astype(BF16)

    pl.semaphore_wait(barrier, 31)

    def send(src, dst, ssem, rsem, device):
        pltpu.make_async_remote_copy(
            src_ref=src, dst_ref=dst, send_sem=ssem, recv_sem=rsem, device_id=device, device_id_type=MESH
        ).start()

    def wait(ref, sem):
        pltpu.make_async_copy(ref, ref, sem).wait()

    class Spread:
        def __init__(self, buf, half, near, mate, ssem, rsem, direct):
            self.buf, self.half, self.near, self.mate = buf, half, near, mate
            self.direct = direct
            self.ssem, self.rsem = ssem, rsem

        def put(self, block, slot, device):
            send(self.buf.at[block], self.buf.at[block], self.ssem, self.rsem(slot), device)

        def put_half(self, block, i, slot, device):
            part_of = self.half(block, i)
            send(part_of, part_of, self.ssem, self.rsem(slot), device)

        def got(self, slot):
            wait(self.buf.at[0], self.rsem(slot))

        def start(self):
            own = y * 2 + self.near
            self.put(own, 1, right)
            self.put(own, 2, left)
            if self.direct:
                self.put(own, 3, right_pair)
                self.put(own, 4, left_pair)
            self.put(own, 0, pair)

        def from_pair(self):
            self.got(0)
            self.put(y * 2 + self.mate, 3, right)
            self.put(y * 2 + self.mate, 4, left)

        def onward(self, which, slot):
            self.got(slot)
            self.put_half(y3 * 2 + which, 0, slot + 4, right)
            self.got(slot + 1)
            self.put_half(y1 * 2 + which, 1, slot + 5, left)

        def second(self):
            self.onward(self.near, 1)

        def third(self):
            self.onward(self.mate, 3)

        def finish(self):
            if self.direct:
                self.got(0)
            for slot in range(5, 9):
                wait(self.half(0, 0), self.rsem(slot))

        def left_here(self):
            wait(self.buf.at[pl.ds(0, 7)], self.ssem)

    for d in FAR_FIRST[:7]:
        send(xz.at[z], xz.at[z], xz_send, xz_recv, z_peer(d))

    loads[1].wait()
    for gg in range(NG):
        for r in range(2):
            mask[gg * ROWS + r * 8 : gg * ROWS + r * 8 + 8, :] = active_ref[
                pl.ds(gg * 2 + r, 8, stride=16), :
            ].astype(F32)

    mine = lax.broadcasted_iota(jnp.int32, (8, 1), 0) == z
    loads[2].wait()

    first_half = (1 - x_hi).astype(F32)

    def goal_rows(target, tile, count, factor=first_half):
        two = goals_ref[target, :, cols(tile, count)].astype(F32) * factor
        zero = jnp.zeros((8, count * LANES), F32)
        return jnp.concatenate([jnp.where(mine, two[r : r + 1], zero) for r in range(2)], axis=0)

    t_a, t_b = 5 * x_hi + core, 2 + 2 * core
    for q, w in enumerate(TILES_OF):
        for zz in range(3):
            goal_block[q][zz] = goal_rows(t_a, 3 * FIRST[q] + w * zz, w, 1.0)
            goal_block[q][zz + 5] = goal_rows(t_b, 3 * FIRST[q] + 1 + w * zz, w)
        goal_block[q][MID] = goal_rows(3, core * 14 + FIRST[q], w)
    goal_block[0][MID + 1] = goal_rows(3, core * 14 + 9, 4)
    goal_block[1][MID + 1, :, 0:LANES] = goal_rows(3, core * 14 + 13, 1)
    goal_block[1][MID + 1, :, LANES : 2 * LANES] = goal_rows(t_a, 27, 1, 1.0)
    goal_block[1][MID + 1, :, 2 * LANES :] = goal_rows(t_b, 0, 1)
    goal_block[2][MID + 1] = jnp.zeros((ROWS, 2 * LANES), F32)

    wait(xz.at[pl.ds(0, 7)], xz_recv)
    for zz in range(NZ):
        xwide[zz * XROWS : (zz + 1) * XROWS, :] = xz[zz].astype(F32)
    for c in range(TILES):
        xb[g, c // 14, :, (c % 14) * LANES : (c % 14 + 1) * LANES] = jnp.concatenate(
            [xwide[pl.ds(2 * c + r, 8, stride=XROWS), :] for r in range(2)], axis=0
        ).astype(BF16)

    x_spread = Spread(xb, lambda b, i: xb.at[b, i], x, 1 - x, xb_send, lambda slot: xb_recv.at[slot], True)
    x_spread.start()
    x_spread.second()
    x_spread.third()
    loads[3].wait()
    loads[4].wait()
    x_spread.finish()

    pre = jnp.dot(xb[:, 0].reshape(TOK, D // 2), enc[: D // 2, :], preferred_element_type=F32)
    pre = pre + jnp.dot(xb[:, 1].reshape(TOK, D // 2), enc[D // 2 :, :], preferred_element_type=F32)
    act = mask[...] * pre
    lat_ref[...] = act.astype(BF16)
    latt_ref[...] = act.T.astype(BF16)

    def decoded(k, tile, count=3):
        return jnp.dot(lat_ref[...], dec[k, :, cols(tile, count)], preferred_element_type=F32)

    def blocks(value):
        return value.reshape(NG, ROWS, value.shape[-1])

    other = (1 - core) * 14
    own = core * 14
    is_a, is_b = send_a.astype(F32), (1 - send_a).astype(F32)
    empty = jnp.zeros((NG, ROWS, 2 * LANES), BF16)

    def cut(value, q, i):
        w = TILES_OF[q] * LANES
        return blocks(value[:, i * w : (i + 1) * w])

    def for_sibling(q):
        w = TILES_OF[q]
        wide = decoded(k_s, first_tile(q, send_a), 3 * w).astype(BF16)
        for i in range(3):
            sib_out[q][i] = cut(wide, q, i)
        sib_out[q][3] = blocks(decoded(k_c, other + FIRST[q], w).astype(BF16))
        if q == 0:
            sib_out[q][4] = blocks(decoded(k_c, other + 9, 4).astype(BF16))
        elif q == 1:
            sib_out[q][4, :, :, 0:LANES] = blocks(decoded(k_c, other + 13, 1).astype(BF16))
            sib_out[q][4, :, :, LANES : 2 * LANES] = blocks((decoded(k_s, 27, 1) * is_a).astype(BF16))
            sib_out[q][4, :, :, 2 * LANES :] = blocks((decoded(k_s, 0, 1) * is_b).astype(BF16))
        else:
            sib_out[q][4] = empty
        send(sib_out[q], sib_in[q], sib_send.at[q], sib_recv.at[q], sibling)

    def own_alone(q):
        wide = decoded(k_n, first_tile(q, 1 - recv_a), 3 * TILES_OF[q]).astype(BF16)
        for i in range(3):
            part[q][:, z_n + i] = cut(wide, q, i)

    def own_shared(q):
        wait(sib_in[q], sib_recv.at[q])
        w = TILES_OF[q]
        wide = decoded(k_r, first_tile(q, recv_a), 3 * w)
        for i in range(3):
            part[q][:, z_r + i] = (cut(wide, q, i) + sib_in[q][i].astype(F32)).astype(BF16)
        part[q][:, MID] = (blocks(decoded(k_c, own + FIRST[q], w)) + sib_in[q][3].astype(F32)).astype(BF16)

        def last(lanes, value):
            part[q][:, MID + 1, :, lanes] = (blocks(value) + sib_in[q][4, :, :, lanes].astype(F32)).astype(BF16)

        if q == 0:
            last(slice(0, 4 * LANES), decoded(k_c, own + 9, 4))
        elif q == 1:
            last(slice(0, LANES), decoded(k_c, own + 13, 1))
            last(slice(LANES, 2 * LANES), decoded(k_a, 27, 1))
            last(slice(2 * LANES, 3 * LANES), decoded(k_b, 0, 1))
        else:
            part[q][:, MID + 1] = empty

    def less_goals(q):
        for zz in range(NZ):
            part[q][g, zz] = (part[q][g, zz].astype(F32) - goal_block[q][zz]).astype(BF16)

    def y_first(q):
        ss = y_send.at[0]
        send(part[q].at[y2 * 2], y_in.at[0], ss, y_recv.at[0, 0], right)
        send(part[q].at[y2 * 2 + 1], y_in.at[1], ss, y_recv.at[0, 1], left)
        send(part[q].at[y1 * 2 + 1], y_in.at[2], ss, y_recv.at[0, 2], right)
        send(part[q].at[y3 * 2], y_in.at[3], ss, y_recv.at[0, 2], left)

    def y_second(q):
        ss = y_send.at[0]
        wait(y_in.at[0], y_recv.at[0, 0])
        for zz in range(NZ):
            part[q][y1 * 2, zz] = (part[q][y1 * 2, zz].astype(F32) + y_in[0, zz].astype(F32)).astype(BF16)
        send(part[q].at[y1 * 2], y_in.at[4], ss, y_recv.at[0, 2], right)
        wait(y_in.at[1], y_recv.at[0, 1])
        for zz in range(NZ):
            part[q][y3 * 2 + 1, zz] = (
                part[q][y3 * 2 + 1, zz].astype(F32) + y_in[1, zz].astype(F32)
            ).astype(BF16)
        send(part[q].at[y3 * 2 + 1], y_in.at[5], ss, y_recv.at[0, 2], left)

    def y_sum(q):
        wait(y_in.at[pl.ds(0, 4)], y_recv.at[0, 2])
        for half, (one, two) in enumerate(((3, 4), (2, 5))):
            here = (x == half).astype(F32)
            for zz in range(NZ):
                part[q][y * 2 + half, zz] = (
                    part[q][y * 2 + half, zz].astype(F32)
                    + y_in[one, zz].astype(F32)
                    + y_in[two, zz].astype(F32)
                    - goal_block[q][zz] * here
                ).astype(BF16)
        send(part[q].at[g_pass], x_in, x_send.at[0], x_recv.at[0], pair)

    def to_z(q):
        for d in FAR_FIRST[:7]:
            send(part[q].at[g_keep, (z + d) % NZ], z_in[q].at[d - 1], z_send.at[q], z_recv.at[q], z_peer(d))

    def x_sum(q):
        wait(x_in, x_recv.at[0])
        for zz in range(NZ):
            part[q][g_keep, zz] = (part[q][g_keep, zz].astype(F32) + x_in[zz].astype(F32)).astype(BF16)
        to_z(q)

    def pair_first():
        less_goals(1)
        for j in (2, 1, 3, 0):
            send(
                part[1].at[((y + j) % 4) * 2 + 1 - keep], pair_in.at[j], x_send.at[1], pair_recv.at[j], pair
            )

    def pair_sum(j):
        wait(pair_in.at[j], pair_recv.at[j])
        to = ((y + j) % 4) * 2 + keep
        for zz in range(NZ):
            part[1][to, zz] = (part[1][to, zz].astype(F32) + pair_in[j, zz].astype(F32)).astype(BF16)

    low, high = pl.ds(0, 4), pl.ds(4, 4)

    def half_first():
        ss = y_send.at[1]
        pair_sum(2)
        send(part[1].at[y2 * 2 + keep, low], half_in.at[0], ss, y_recv.at[1, 0], right)
        send(part[1].at[y2 * 2 + keep, high], half_in.at[1], ss, y_recv.at[1, 1], left)
        pair_sum(1)
        send(part[1].at[y1 * 2 + keep, high], half_in.at[2], ss, y_recv.at[1, 2], right)
        pair_sum(3)
        send(part[1].at[y3 * 2 + keep, low], half_in.at[3], ss, y_recv.at[1, 2], left)
        pair_sum(0)

    def half_second():
        ss = y_send.at[1]
        wait(half_in.at[0], y_recv.at[1, 0])
        to = y1 * 2 + keep
        for zz in range(4):
            part[1][to, zz] = (part[1][to, zz].astype(F32) + half_in[0, zz].astype(F32)).astype(BF16)
        send(part[1].at[to, low], half_in.at[4], ss, y_recv.at[1, 2], right)
        wait(half_in.at[1], y_recv.at[1, 1])
        to = y3 * 2 + keep
        for zz in range(4):
            part[1][to, zz + 4] = (part[1][to, zz + 4].astype(F32) + half_in[1, zz].astype(F32)).astype(BF16)
        send(part[1].at[to, high], half_in.at[5], ss, y_recv.at[1, 2], left)

    def half_sum():
        wait(half_in.at[pl.ds(0, 4)], y_recv.at[1, 2])
        for at, one, two in ((0, 3, 4), (4, 2, 5)):
            for zz in range(4):
                part[1][g_keep, at + zz] = (
                    part[1][g_keep, at + zz].astype(F32)
                    + half_in[one, zz].astype(F32)
                    + half_in[two, zz].astype(F32)
                ).astype(BF16)
        to_z(1)

    def z_sum(q):
        wait(z_in[q], z_recv.at[q])
        total = part[q][g_keep, z].astype(F32)
        for i in range(7):
            total = total + z_in[q][i].astype(F32)
        value = (total * scale).astype(BF16)
        term[q][...] = value
        err[q][g_keep, z] = value
        own = term[q]
        for d in FAR_FIRST[:7]:
            send(own, err[q].at[g_keep, z], ez_send.at[q], ez_recv.at[q], z_peer(d))

        @pl.when(z >= 3)
        def _():
            for d in FAR_FIRST:
                send(own, err_far[q].at[z - 3], ef_send.at[q], ef_recv.at[q], across_z(d))

    def bulk_first():
        less_goals(2)
        for d in FAR_FIRST[:7]:
            send(part[2].at[:, (z + d) % NZ], bulk_in.at[d - 1], bulk_send.at[0], bulk_recv.at[0], z_peer(d))

    def bulk_sum():
        wait(bulk_in, bulk_recv.at[0])
        for gg in range(NG):
            total = part[2][gg, z].astype(F32)
            for i in range(7):
                total = total + bulk_in[i, gg].astype(F32)
            part[2][gg, z] = total.astype(BF16)
        for d in range(1, 8):
            send(
                part[2].at[(g + d) % NG, z], plane_in.at[d - 1], plane_send.at[0], plane_recv.at[0], plane_peer(d)
            )

    def plane_sum():
        wait(plane_in, plane_recv.at[0])
        total = part[2][g, z].astype(F32)
        for i in range(7):
            total = total + plane_in[i].astype(F32)
        value = (total * scale).astype(BF16)
        term[2][...] = value
        err[2][g, z] = value
        own = term[2]
        for d in range(1, 8):
            send(own, err[2].at[g, z], plane_send.at[1], plane_recv.at[1], plane_peer(d))

        @pl.when(z >= 3)
        def _():
            for d in FAR_FIRST:
                send(own, plane_far.at[g], far_send, far_recv, across_plane(d))

    def plane_spread():
        wait(plane_in, plane_recv.at[1])

        @pl.when(z >= 3)
        def _():
            wait(plane_far, far_recv)
            for gg in range(NG):
                err[2][gg, z] = (err[2][gg, z].astype(F32) + plane_far[gg].astype(F32)).astype(BF16)

        for d in FAR_FIRST[:7]:
            send(err[2].at[:, z], err[2].at[:, z], bulk_send.at[1], bulk_recv.at[1], z_peer(d))

    def to_sibling(q):
        send(err[q].at[:, pl.ds(z_r, 3)], err_sib[q].at[:, pl.ds(0, 3)], es_send.at[q], es_recv.at[q], sibling)
        send(err[q].at[:, pl.ds(3, 2)], err_sib[q].at[:, pl.ds(3, 2)], es_send.at[q], es_recv.at[q], sibling)

    def bulk_arrived():
        wait(bulk_in, bulk_recv.at[1])
        to_sibling(2)

    y_spread = Spread(
        err[0],
        lambda b, i: err[0].at[b, pl.ds(4 * i, 4)],
        keep,
        1 - keep,
        ep_send.at[0],
        lambda slot: ep_recv.at[0, slot],
        False,
    )

    class HalfSpread:
        def put(self, block, which, slot, device):
            at = err[1].at[block] if which is None else err[1].at[block, which]
            send(at, at, ep_send.at[1], ep_recv.at[1, slot], device)

        def got(self, slot, which=None):
            wait(err[1].at[0] if which is None else err[1].at[0, which], ep_recv.at[1, slot])

        def start(self):
            self.put(g_keep, None, 0, right)
            self.put(g_keep, None, 1, left)
            self.put(g_keep, None, 4, pair)

        def second(self):
            self.got(0)
            self.put(y3 * 2 + keep, low, 2, right)
            self.put(y3 * 2 + keep, None, 5, pair)
            self.got(1)
            self.put(y1 * 2 + keep, high, 3, left)
            self.put(y1 * 2 + keep, None, 6, pair)

        def third(self):
            self.got(2, low)
            self.put(y2 * 2 + keep, low, 7, pair)
            self.got(3, high)
            self.put(y2 * 2 + keep, high, 8, pair)

        def finish(self):
            for slot in (4, 5, 6):
                self.got(slot)
            self.got(7, low)
            self.got(8, high)

        def left_here(self):
            wait(err[1].at[pl.ds(0, 7)], ep_send.at[1])

    spreads = [y_spread, HalfSpread()]

    def z_spread(q):
        wait(err[q].at[0, pl.ds(0, 7)], ez_recv.at[q])
        wait(err_far[q], ef_recv.at[q])
        for zz in range(3, NZ):
            far = err_far[q][zz - 3].astype(F32)
            if q == 1 and zz == 4:
                tile = lax.broadcasted_iota(jnp.int32, (ROWS, 3 * LANES), 1) // LANES
                far = jnp.where(tile == 1, 0.0, far)
            err[q][g_keep, zz] = (err[q][g_keep, zz].astype(F32) + far).astype(BF16)
        spreads[q].start()

    def arrived(q):
        spreads[q].finish()
        to_sibling(q)

    def backward(error, k, tile, count=3):
        where = cols(tile, count)
        dlat_ref[...] += lax.dot_general(
            error, dec[k, :, where], (((1,), (1,)), ((), ())), preferred_element_type=F32
        )
        gdec[k, :, where] = jnp.dot(latt_ref[...], error, preferred_element_type=F32).astype(BF16)

    def whole(value):
        return value.reshape(TOK, value.shape[-1])

    def wide(ref, q, at):
        return jnp.concatenate([whole(ref[q][:, at + i]) for i in range(3)], axis=1)

    def own_back(q):
        w = TILES_OF[q]
        backward(wide(err, q, 0), k_a, first_tile(q, 1), 3 * w)
        backward(wide(err, q, 5), k_b, first_tile(q, 0), 3 * w)
        backward(whole(err[q][:, MID]), k_c, own + FIRST[q], w)
        if q == 0:
            backward(whole(err[q][:, MID + 1]), k_c, own + 9, 4)
        elif q == 1:
            backward(whole(err[q][:, MID + 1, :, 0:LANES]), k_c, own + 13, 1)
            backward(whole(err[q][:, MID + 1, :, LANES : 2 * LANES]), k_a, 27, 1)
            backward(whole(err[q][:, MID + 1, :, 2 * LANES :]), k_b, 0, 1)

    def sibling_back(q):
        wait(err_sib[q], es_recv.at[q])
        w = TILES_OF[q]
        backward(wide(err_sib, q, 0), k_s, first_tile(q, send_a), 3 * w)
        backward(whole(err_sib[q][:, 3]), k_c, other + FIRST[q], w)
        if q == 0:
            backward(whole(err_sib[q][:, 4]), k_c, other + 9, 4)
        elif q == 1:
            backward(whole(err_sib[q][:, 4, :, 0:LANES]), k_c, other + 13, 1)
            lanes = pl.ds(pl.multiple_of((2 - send_a) * LANES, LANES), LANES)
            backward(whole(err_sib[q][:, 4, :, lanes]), k_s, 27 * send_a, 1)

    for_sibling(1)
    for_sibling(0)
    own_alone(1)
    own_shared(1)
    pair_first()
    for_sibling(2)
    own_alone(0)
    own_shared(0)
    y_first(0)
    own_alone(2)
    own_shared(2)
    bulk_first()
    y_second(0)
    half_first()
    half_second()
    y_sum(0)
    half_sum()
    x_sum(0)
    for c in range(TILES):
        block = xb[:, c // 14, :, (c % 14) * LANES : (c % 14 + 1) * LANES].reshape(TOK, LANES)
        xt[c * LANES : (c + 1) * LANES, :] = block.T
    dlat_ref[...] = jnp.zeros_like(dlat_ref)
    bulk_sum()
    z_sum(1)
    plane_sum()
    z_sum(0)
    plane_spread()
    z_spread(1)
    z_spread(0)
    spreads[1].second()
    spreads[0].from_pair()
    spreads[1].third()
    spreads[0].second()
    spreads[0].third()
    arrived(1)
    bulk_arrived()
    own_back(1)
    own_back(2)
    sibling_back(1)
    arrived(0)
    own_back(0)
    sibling_back(2)
    sibling_back(0)

    wait(xz.at[pl.ds(0, 7)], xz_send)
    x_spread.left_here()
    for q in range(NQ):
        wait(sib_in[q], sib_send.at[q])
        wait(err_sib[q], es_send.at[q])
    for q in range(2):
        wait(z_in[q], z_send.at[q])
        wait(z_in[q], ez_send.at[q])
        spreads[q].left_here()
    wait(y_in, y_send.at[0])
    wait(half_in, y_send.at[1])
    wait(x_in, x_send.at[0])
    wait(pair_in, x_send.at[1])
    for i in range(2):
        wait(bulk_in, bulk_send.at[i])
        wait(plane_in, plane_send.at[i])

    @pl.when(z >= 3)
    def _():
        for q in range(2):
            wait(err[q].at[0], ef_send.at[q])
        wait(plane_far, far_send)


def last_kernel(gdec, xt, mask, dlat, genc_hbm, gdec_hbm, genc, sem):
    gdec_copy = pltpu.make_async_copy(gdec, gdec_hbm.at[0], sem.at[0])
    gdec_copy.start()
    dpre = (mask[...] * dlat[...]).astype(BF16)
    genc[...] = jnp.dot(xt[...], dpre, preferred_element_type=F32).astype(BF16)
    genc_copy = pltpu.make_async_copy(genc, genc_hbm.at[0], sem.at[1])
    genc_copy.start()
    gdec_copy.wait()
    genc_copy.wait()


def local(inputs, encoder, active, decoder, goals):
    vmem = pl.BlockSpec(memory_space=pltpu.VMEM)
    hbm = pl.BlockSpec(memory_space=pl.ANY)
    dma = pltpu.SemaphoreType.DMA
    per_q = [dma((NQ,))] * 2

    def chunk(q, shape, dtype=BF16):
        return pltpu.VMEM((*shape, TILES_OF[q] * LANES), dtype)

    def chunks(shape, dtype=BF16):
        return [chunk(q, shape, dtype) for q in range(NQ)]

    gdec, xt, mask, dlat = pl.pallas_call(
        kernel,
        out_shape=(
            pltpu.VMEM((4, FL, D), BF16),
            pltpu.VMEM((D, TOK), BF16),
            pltpu.VMEM((TOK, FL), F32),
            pltpu.VMEM((TOK, FL), F32),
        ),
        in_specs=[pl.BlockSpec(memory_space=pltpu.HBM)] * 5,
        out_specs=[vmem] * 4,
        scratch_shapes=[
            pltpu.VMEM((2, D), BF16),
            pltpu.VMEM((7, 2, D), BF16),
            pltpu.VMEM((TOK, FL), jnp.int32),
            pltpu.VMEM((D, FL), BF16),
            pltpu.VMEM((4, FL, D), BF16),
            pltpu.VMEM((XROWS, LANES), F32),
            pltpu.VMEM((NZ, XROWS, LANES), BF16),
            pltpu.VMEM((NZ * XROWS, LANES), F32),
            pltpu.VMEM((NG, 2, ROWS, D // 2), BF16),
            pltpu.VMEM((TOK, FL), BF16),
            pltpu.VMEM((FL, TOK), BF16),
            chunks((NZ, ROWS), F32),
            chunks((5, NG, ROWS)),
            chunks((5, NG, ROWS)),
            chunks((NG, NZ, ROWS)),
            chunk(0, (6, NZ, ROWS)),
            chunk(1, (6, 4, ROWS)),
            chunk(1, (4, NZ, ROWS)),
            chunk(0, (NZ, ROWS)),
            chunks((NZ - 1, ROWS))[:2],
            chunk(2, (NZ - 1, NG, ROWS)),
            chunk(2, (NG - 1, ROWS)),
            chunks((ROWS,)),
            chunks((NG, NZ, ROWS)),
            chunks((5, ROWS))[:2],
            chunk(2, (NG, ROWS)),
            chunks((NG, 5, ROWS)),
            dma((5,)),
            dma,
            dma,
            dma,
            dma((9,)),
            *per_q,
            dma((NQ,)),
            dma((NQ, 3)),
            *per_q,
            dma((4,)),
            *per_q,
            *per_q,
            *per_q,
            dma((NQ,)),
            dma((NQ, 9)),
            *per_q,
            dma((2,)),
            dma((2,)),
            dma((2,)),
            dma((2,)),
            dma,
            dma,
        ],
        compiler_params=pltpu.CompilerParams(
            collective_id=0, has_side_effects=True, vmem_limit_bytes=54 * 2**20
        ),
        name="step",
    )(inputs, goals, active, encoder, decoder)
    return pl.pallas_call(
        last_kernel,
        out_shape=(
            jax.ShapeDtypeStruct((1, D, FL), BF16),
            jax.ShapeDtypeStruct((1, 4, FL, D), BF16),
        ),
        in_specs=[vmem] * 4,
        out_specs=(hbm, hbm),
        scratch_shapes=[pltpu.VMEM((D, FL), BF16), dma((2,))],
        compiler_params=pltpu.CompilerParams(vmem_limit_bytes=8 * 2**20),
        name="write",
    )(gdec, xt, mask, dlat)


def solution(mesh):
    return jax.shard_map(
        local,
        mesh=mesh,
        in_specs=(
            P("layer", "slab", None),
            P("layer", None, "slab"),
            P("layer", None, "slab"),
            P("layer", None, "slab", None),
            P(None, "slab", None),
        ),
        out_specs=(P("layer", None, "slab"), P("layer", None, "slab", None)),
        check_vma=False,
    )
```

time: 91.9 us -> 83.6 us (0.910)
  Pallas kernels: 91.1 us -> 82.8 us
    pallas_call x1, Pallas kernels: 89 us -> 80.6 us  [local(): pl.pallas_call(kernel, out_shape=(pltpu.VMEM((4, FL, D), BF16), pltpu.VME...]
where the time goes in v3:
time: 83.6 us; the launch traced here: 83.4 us
  Pallas kernels  82.8 us (99%)
    pallas_call x1, Pallas kernels, local(): pl.pallas_call(kernel, out_shape=(pltpu.VMEM((4, FL, D), BF16), pltpu.VME...  80.6 us
    pallas_call x1, Pallas kernels, local(): pl.pallas_call(last_kernel, out_shape=(jax.ShapeDtypeStruct((1, D, FL), B...  2.15 us

profile of v3, /device:TPU:1, one launch (start us, length us, event | category | flops | bytes accessed | tf_op | source)
XLA Modules:
  0.0 83.4 jit_solution(9536489220643882193)
XLA Ops:
  0.6 80.6 %step.1 = (bf16[4,128,3584]{2,1,0:T(8,128)(2,1)S(1)}, bf16[3584,128]{1,0:T(8,128)(2,1)S(1)}, f32[128,128]{1,0:T(8,128)S(1)}, f32[128,128]{1,0:T(8,128)S(1)}) custom-call(bf16[1,2,3584]{2,1,0:T(2,128)(2,1)} %inputs_hbm.1, bf16[7,2,3584]{2,1,0:T(2,128)(2,1)} %goals_hbm.1, s32[1,128,128]{2,1,0:T(8,128)} %active_hbm.1, bf16[1,3584,128]{2,1,0:T(8,128)(2,1)} %enc_hbm.1, ...), custom_call_target="tpu_custom_call" | custom-call | tf_op jit(solution)/shard_map/step/pallas_call | solution.py:702
  81.2 2.1 %write.1 = (bf16[1,3584,128]{2,1,0:T(8,128)(2,1)}, bf16[1,4,128,3584]{3,2,1,0:T(8,128)(2,1)}) custom-call(bf16[4,128,3584]{2,1,0:T(8,128)(2,1)S(1)} %get-tuple-element.6.gdec, bf16[3584,128]{1,0:T(8,128)(2,1)S(1)} %get-tuple-element.7.xt, f32[128,128]{1,0:T(8,128)S(1)} %get-tuple-element.8.mask, f32[128,128]{1,0:T(8,128)S(1)} %get-tuple-element.9.dlat), custom_call_target="tpu_custom_call" | custom-call | tf_op jit(solution)/shard_map/write/pallas_call | solution.py:768

commit v4 on v3

--- a/solution.py
+++ b/solution.py
@@ -135,6 +135,19 @@
     def first_tile(q, is_a):
         return 3 * FIRST[q] + 1 - is_a
 
+    barrier = pltpu.get_barrier_semaphore()
+
+    def greet(device):
+        pl.semaphore_signal(barrier, inc=1, device_id=device, device_id_type=MESH)
+
+    for d in FAR_FIRST:
+        greet(across_z(d))
+        greet(across_plane(d))
+        if d:
+            greet(z_peer(d))
+            greet(plane_peer(d))
+    greet(sibling)
+
     loads = [
         pltpu.make_async_copy(src, dst, load_sem.at[i])
         for i, (src, dst) in enumerate(
@@ -150,19 +163,6 @@
     for load in loads:
         load.start()
 
-    barrier = pltpu.get_barrier_semaphore()
-
-    def greet(device):
-        pl.semaphore_signal(barrier, inc=1, device_id=device, device_id_type=MESH)
-
-    for d in FAR_FIRST:
-        greet(across_z(d))
-        greet(across_plane(d))
-        if d:
-            greet(z_peer(d))
-            greet(plane_peer(d))
-    greet(sibling)
-
     xstage[...] = jnp.zeros_like(xstage)
     loads[0].wait()
     for c in range(TILES):
@@ -221,11 +221,17 @@
         def third(self):
             self.onward(self.mate, 3)
 
-        def finish(self):
+        def near_rows(self):
             if self.direct:
                 self.got(0)
+
+        def far_row(self):
             for slot in range(5, 9):
                 wait(self.half(0, 0), self.rsem(slot))
+
+        def finish(self):
+            self.near_rows()
+            self.far_row()
 
         def left_here(self):
             wait(self.buf.at[pl.ds(0, 7)], self.ssem)
@@ -402,16 +408,18 @@
 
     low, high = pl.ds(0, 4), pl.ds(4, 4)
 
-    def half_first():
+    def half_far():
         ss = y_send.at[1]
         pair_sum(2)
         send(part[1].at[y2 * 2 + keep, low], half_in.at[0], ss, y_recv.at[1, 0], right)
         send(part[1].at[y2 * 2 + keep, high], half_in.at[1], ss, y_recv.at[1, 1], left)
+
+    def half_near():
+        ss = y_send.at[1]
         pair_sum(1)
         send(part[1].at[y1 * 2 + keep, high], half_in.at[2], ss, y_recv.at[1, 2], right)
         pair_sum(3)
         send(part[1].at[y3 * 2 + keep, low], half_in.at[3], ss, y_recv.at[1, 2], left)
-        pair_sum(0)
 
     def half_second():
         ss = y_send.at[1]
@@ -427,6 +435,7 @@
         send(part[1].at[to, high], half_in.at[5], ss, y_recv.at[1, 2], left)
 
     def half_sum():
+        pair_sum(0)
         wait(half_in.at[pl.ds(0, 4)], y_recv.at[1, 2])
         for at, one, two in ((0, 3, 4), (4, 2, 5)):
             for zz in range(4):
@@ -545,9 +554,11 @@
             self.got(3, high)
             self.put(y2 * 2 + keep, high, 8, pair)
 
-        def finish(self):
+        def near_rows(self):
             for slot in (4, 5, 6):
                 self.got(slot)
+
+        def far_row(self):
             self.got(7, low)
             self.got(8, high)
 
@@ -567,9 +578,19 @@
             err[q][g_keep, zz] = (err[q][g_keep, zz].astype(F32) + far).astype(BF16)
         spreads[q].start()
 
+    def row_to_sibling(q, row):
+        rows = pl.ds(2 * row, 2)
+        send(err[q].at[rows, pl.ds(z_r, 3)], err_sib[q].at[rows, pl.ds(0, 3)], es_send.at[q], es_recv.at[q], sibling)
+        send(err[q].at[rows, pl.ds(3, 2)], err_sib[q].at[rows, pl.ds(3, 2)], es_send.at[q], es_recv.at[q], sibling)
+
+    def near_arrived(q):
+        spreads[q].near_rows()
+        for row in (y, y1, y3):
+            row_to_sibling(q, row)
+
     def arrived(q):
-        spreads[q].finish()
-        to_sibling(q)
+        spreads[q].far_row()
+        row_to_sibling(q, y2)
 
     def backward(error, k, tile, count=3):
         where = cols(tile, count)
@@ -620,8 +641,9 @@
     own_alone(2)
     own_shared(2)
     bulk_first()
+    half_far()
+    half_near()
     y_second(0)
-    half_first()
     half_second()
     y_sum(0)
     half_sum()
@@ -630,18 +652,20 @@
         block = xb[:, c // 14, :, (c % 14) * LANES : (c % 14 + 1) * LANES].reshape(TOK, LANES)
         xt[c * LANES : (c + 1) * LANES, :] = block.T
     dlat_ref[...] = jnp.zeros_like(dlat_ref)
+    z_sum(1)
     bulk_sum()
-    z_sum(1)
+    z_sum(0)
     plane_sum()
-    z_sum(0)
-    plane_spread()
     z_spread(1)
     z_spread(0)
+    plane_spread()
     spreads[1].second()
     spreads[0].from_pair()
     spreads[1].third()
+    near_arrived(1)
     spreads[0].second()
     spreads[0].third()
+    near_arrived(0)
     arrived(1)
     bulk_arrived()
     own_back(1)

time: 83.6 us -> 83.6 us (level)
  no operation moved by 1% of the time
where the time goes in v4:
time: 83.6 us; the launch traced here: 83.5 us
  Pallas kernels  82.8 us (99%)
    pallas_call x1, Pallas kernels, local(): pl.pallas_call(kernel, out_shape=(pltpu.VMEM((4, FL, D), BF16), pltpu.VME...  80.7 us
    pallas_call x1, Pallas kernels, local(): pl.pallas_call(last_kernel, out_shape=(jax.ShapeDtypeStruct((1, D, FL), B...  2.15 us

profile of v4, /device:TPU:1, one launch (start us, length us, event | category | flops | bytes accessed | tf_op | source)
XLA Modules:
  0.0 83.5 jit_solution(17516378889776287484)
XLA Ops:
  0.6 80.7 %step.1 = (bf16[4,128,3584]{2,1,0:T(8,128)(2,1)S(1)}, bf16[3584,128]{1,0:T(8,128)(2,1)S(1)}, f32[128,128]{1,0:T(8,128)S(1)}, f32[128,128]{1,0:T(8,128)S(1)}) custom-call(bf16[1,2,3584]{2,1,0:T(2,128)(2,1)} %inputs_hbm.1, bf16[7,2,3584]{2,1,0:T(2,128)(2,1)} %goals_hbm.1, s32[1,128,128]{2,1,0:T(8,128)} %active_hbm.1, bf16[1,3584,128]{2,1,0:T(8,128)(2,1)} %enc_hbm.1, ...), custom_call_target="tpu_custom_call" | custom-call | tf_op jit(solution)/shard_map/step/pallas_call | solution.py:726
  81.3 2.1 %write.1 = (bf16[1,3584,128]{2,1,0:T(8,128)(2,1)}, bf16[1,4,128,3584]{3,2,1,0:T(8,128)(2,1)}) custom-call(bf16[4,128,3584]{2,1,0:T(8,128)(2,1)S(1)} %get-tuple-element.6.gdec, bf16[3584,128]{1,0:T(8,128)(2,1)S(1)} %get-tuple-element.7.xt, f32[128,128]{1,0:T(8,128)S(1)} %get-tuple-element.8.mask, f32[128,128]{1,0:T(8,128)S(1)} %get-tuple-element.9.dlat), custom_call_target="tpu_custom_call" | custom-call | tf_op jit(solution)/shard_map/write/pallas_call | solution.py:792
